TPU v7x, 32 devices: a whole 2x2x4 slice. The times are simulated.
32 devices in a mesh: section: 2 (over x), rows: 16 (over z, y, core).
Axes of the slice: x: 2, y: 2, z: 4, core: 2. Of those that a mesh axis runs over, the one named last changes fastest.
Arguments:
- section_input: bfloat16 [2, 32, 512, 768], P('section', 'rows'), may hold values from -6 to 6
- enc_lengths: int32 [32, 4], P('rows'), may hold values from 1 to 256, 512 in all within a row
- dec_lengths: int32 [32, 4], P('rows'), may hold values from 1 to 128, 256 in all within a row
- attn_in: bfloat16 [2, 768, 2304], P('section'), may hold values from -0.21875 to 0.21875
- attn_out: bfloat16 [2, 768, 768], P('section'), may hold values from -1.25 to 1.25
- ffn_in: bfloat16 [2, 768, 4096], P('section'), may hold values from -0.21875 to 0.21875
- ffn_out: bfloat16 [2, 2048, 768], P('section'), may hold values from -0.125 to 0.125
- cross_weight: bfloat16 [2, 768, 1536], P('section'), may hold values from -8 to 8
- gains: float32 [2, 3, 768], P('section'), may hold values from 0.5 to 1.5
Outputs:
- results: float32 [2, 32, 512, 768], P('section', 'rows')
- grad_attn_in: float32 [2, 768, 2304], P('section', 'rows')
- grad_attn_out: float32 [2, 768, 768], P('section', 'rows')
- grad_ffn_in: float32 [2, 768, 4096], P('section', 'rows')
- grad_ffn_out: float32 [2, 2048, 768], P('section', 'rows')
- grad_cross: float32 [2, 768, 1536], P('section', 'rows')
- grad_gains: float32 [2, 3, 768], P('section', None, 'rows')
Inputs may be any that keep to these rules, and one draw needn't show every extreme that they name: `enc_lengths`: the 4 lengths of a row sum to 512; the largest in each row is half of 512. Decoder document j belongs to encoder document j. `dec_lengths`: the 4 lengths of a row sum to 256; the largest in each row is half of 256.
All inputs are finite; a program needn't handle non-finite values.
Results may differ from a plain program's by a relative error of at most 0.02.
Values may be sent and summed in bfloat16 or wider, within the bound.
A program may use at most 320 MiB of HBM per device.

v0:
```python
import functools

import jax
import jax.numpy as jnp
from jax import lax
from jax.sharding import PartitionSpec as P

HEADS = 12
MICRO = 2


EPSILON = 1e-06
SCALE = 0.125
NEGATIVE = -1e30


def from_behind(x, axis, by):
    peers = lax.axis_size(axis)
    pairs = [(i, i + by) for i in range(peers) if 0 <= i + by < peers]
    return lax.ppermute(x, axis, pairs)


def rms_norm(value_in, gain_in):
    return (
        value_in * lax.rsqrt(jnp.mean(value_in * value_in, -1, keepdims=True) + EPSILON) * gain_in
    )


def activate(gate_up, split_at):
    return jax.nn.gelu(gate_up[..., :split_at], approximate=True) * gate_up[..., split_at:]


def project(left_op, right_op):
    return jnp.einsum("rld,de->rle", left_op, right_op, preferred_element_type=jnp.float32)


def project_back(grad_in, right_op):
    return jnp.einsum("rle,de->rld", grad_in, right_op, preferred_element_type=jnp.float32)


def outer_sum(left_op, grad_in):
    return jnp.einsum("rld,rle->de", left_op, grad_in, preferred_element_type=jnp.float32)


def segment_ids(lengths, span_len):
    seg_ends = jnp.cumsum(lengths, -1, dtype=jnp.int32)
    positions = jnp.arange(span_len, dtype=jnp.int32)
    return jnp.sum(
        (positions[None, :, None] >= seg_ends[:, None, :]).astype(jnp.int32), -1, dtype=jnp.int32
    )


def split_heads(value_in, head_count):
    return value_in.reshape(value_in.shape[0], value_in.shape[1], head_count, -1)


def attn_scores(queries, keys_in, allowed, head_count):
    scores = (
        jnp.einsum(
            "rqhd,rkhd->rhqk",
            split_heads(queries, head_count),
            split_heads(keys_in, head_count),
            preferred_element_type=jnp.float32,
        )
        * SCALE
    )
    return jnp.where(allowed[:, None], scores, NEGATIVE)


def attention_forward(queries, keys_in, values_in, allowed, head_count):
    scores = attn_scores(queries, keys_in, allowed, head_count)
    row_max = jnp.max(scores, -1, keepdims=True)
    shifted_exp = jnp.exp(scores - row_max)
    row_sum = jnp.sum(shifted_exp, -1, keepdims=True)
    attn_probs = (shifted_exp / row_sum).astype(jnp.bfloat16)
    attn_mixed = jnp.einsum(
        "rhqk,rkhd->rqhd",
        attn_probs,
        split_heads(values_in, head_count),
        preferred_element_type=jnp.float32,
    )
    return (attn_mixed.reshape(queries.shape).astype(jnp.bfloat16), row_max + jnp.log(row_sum))


def attention_backward(queries, keys_in, values_in, allowed, log_total, grad_mixed, head_count):
    attn_probs = jnp.exp(attn_scores(queries, keys_in, allowed, head_count) - log_total)
    grad_heads = split_heads(grad_mixed, head_count)
    grad_probs = jnp.einsum(
        "rqhd,rkhd->rhqk",
        grad_heads,
        split_heads(values_in, head_count),
        preferred_element_type=jnp.float32,
    )
    grad_values = jnp.einsum(
        "rhqk,rqhd->rkhd",
        attn_probs.astype(jnp.bfloat16),
        grad_heads,
        preferred_element_type=jnp.float32,
    )
    grad_scores = (
        attn_probs * (grad_probs - jnp.sum(attn_probs * grad_probs, -1, keepdims=True))
    ).astype(jnp.bfloat16)
    grad_queries = (
        jnp.einsum(
            "rhqk,rkhd->rqhd",
            grad_scores,
            split_heads(keys_in, head_count),
            preferred_element_type=jnp.float32,
        )
        * SCALE
    )
    grad_keys = (
        jnp.einsum(
            "rhqk,rqhd->rkhd",
            grad_scores,
            split_heads(queries, head_count),
            preferred_element_type=jnp.float32,
        )
        * SCALE
    )
    return (
        grad_queries.reshape(queries.shape),
        grad_keys.reshape(keys_in.shape),
        grad_values.reshape(values_in.shape),
    )


def self_forward(hidden, gain_in, w_in, w_out, allowed, head_count):
    att_width = w_out.shape[0]
    normed = rms_norm(hidden, gain_in).astype(jnp.bfloat16)
    packed = project(normed, w_in).astype(jnp.bfloat16)
    attn_mixed, log_total = attention_forward(
        packed[..., :att_width],
        packed[..., att_width : 2 * att_width],
        packed[..., 2 * att_width :],
        allowed,
        head_count,
    )
    return (hidden + project(attn_mixed, w_out), (normed, packed, attn_mixed, log_total))


def self_backward(hidden, gain_in, w_in, w_out, allowed, head_count, kept, grad_out):
    normed, packed, attn_mixed, log_total = kept
    att_width = w_out.shape[0]
    grad_branch = grad_out.astype(jnp.bfloat16)
    grad_w_out = outer_sum(attn_mixed, grad_branch)
    grad_mixed = project_back(grad_branch, w_out).astype(jnp.bfloat16)
    grad_q, grad_k, grad_v = attention_backward(
        packed[..., :att_width],
        packed[..., att_width : 2 * att_width],
        packed[..., 2 * att_width :],
        allowed,
        log_total,
        grad_mixed,
        head_count,
    )
    grad_packed = jnp.concatenate([grad_q, grad_k, grad_v], -1).astype(jnp.bfloat16)
    grad_w_in = outer_sum(normed, grad_packed)
    grad_normed = project_back(grad_packed, w_in)
    _, norm_pull = jax.vjp(rms_norm, hidden, gain_in)
    grad_hidden, grad_gain = norm_pull(grad_normed)
    return (grad_out + grad_hidden, grad_w_in, grad_w_out, grad_gain)


def ffn_forward(hidden, gain_in, w_in, w_out):
    normed = rms_norm(hidden, gain_in).astype(jnp.bfloat16)
    gate_up = project(normed, w_in)
    activated = activate(gate_up, w_out.shape[0]).astype(jnp.bfloat16)
    return (hidden + project(activated, w_out), (normed, gate_up, activated))


def ffn_backward(hidden, gain_in, w_in, w_out, kept, grad_out):
    normed, gate_up, activated = kept
    grad_branch = grad_out.astype(jnp.bfloat16)
    grad_w_out = outer_sum(activated, grad_branch)
    grad_inner = project_back(grad_branch, w_out)
    _, gate_pull = jax.vjp(functools.partial(activate, split_at=w_out.shape[0]), gate_up)
    grad_gate_up = gate_pull(grad_inner)[0].astype(jnp.bfloat16)
    grad_w_in = outer_sum(normed, grad_gate_up)
    grad_normed = project_back(grad_gate_up, w_in)
    _, norm_pull = jax.vjp(rms_norm, hidden, gain_in)
    grad_hidden, grad_gain = norm_pull(grad_normed)
    return (grad_out + grad_hidden, grad_w_in, grad_w_out, grad_gain)


def encoder_trunk(hidden, weights, seg_rows, head_count):
    attn_in, attn_out, ffn_in, ffn_out, cross_weight, gains = weights
    allowed = seg_rows[:, :, None] == seg_rows[:, None, :]
    after_attn, kept_attn = self_forward(hidden, gains[0], attn_in, attn_out, allowed, head_count)
    after_ffn, kept_ffn = ffn_forward(after_attn, gains[2], ffn_in, ffn_out)
    memory = rms_norm(after_ffn, gains[1]).astype(jnp.bfloat16)
    return (memory, (allowed, after_attn, after_ffn, kept_attn, kept_ffn))


def encoder_backward(hidden, weights, seg_rows, head_count, grad_sent):
    attn_in, attn_out, ffn_in, ffn_out, cross_weight, gains = weights
    memory, kept = encoder_trunk(hidden, weights, seg_rows, head_count)
    allowed, after_attn, after_ffn, kept_attn, kept_ffn = kept
    grad_cross = outer_sum(memory, grad_sent)
    grad_memory = project_back(grad_sent, cross_weight)
    _, norm_pull = jax.vjp(rms_norm, after_ffn, gains[1])
    grad_after_ffn, grad_final = norm_pull(grad_memory)
    grad_after_attn, grad_fi, grad_fo, grad_ffn_gain = ffn_backward(
        after_attn, gains[2], ffn_in, ffn_out, kept_ffn, grad_after_ffn
    )
    grad_hidden, grad_ai, grad_ao, grad_attn_gain = self_backward(
        hidden, gains[0], attn_in, attn_out, allowed, head_count, kept_attn, grad_after_attn
    )
    return (
        grad_hidden,
        (
            grad_ai,
            grad_ao,
            grad_fi,
            grad_fo,
            grad_cross,
            jnp.stack([grad_attn_gain, grad_final, grad_ffn_gain]),
        ),
    )


def decoder_pass(hidden, grad_out, sent_kv, weights, seg_rows, seg_other, head_count):
    attn_in, attn_out, ffn_in, ffn_out, cross_weight, gains = weights
    att_width = attn_out.shape[0]
    positions = jnp.arange(hidden.shape[1], dtype=jnp.int32)
    allowed = (seg_rows[:, :, None] == seg_rows[:, None, :]) & (
        positions[None, None, :] <= positions[None, :, None]
    )
    across = seg_rows[:, :, None] == seg_other[:, None, :]
    after_self, kept_attn = self_forward(hidden, gains[0], attn_in, attn_out, allowed, head_count)
    normed = rms_norm(after_self, gains[1]).astype(jnp.bfloat16)
    query_proj = cross_weight[:, :att_width]
    out_proj = cross_weight[:, att_width:]
    queries = project(normed, query_proj).astype(jnp.bfloat16)
    keys_in = sent_kv[..., :att_width]
    values_in = sent_kv[..., att_width:]
    attn_mixed, log_total = attention_forward(queries, keys_in, values_in, across, head_count)
    after_cross = after_self + jnp.einsum(
        "rqe,de->rqd", attn_mixed, out_proj, preferred_element_type=jnp.float32
    )
    output, kept_ffn = ffn_forward(after_cross, gains[2], ffn_in, ffn_out)
    grad_cross_out, grad_fi, grad_fo, grad_ffn_gain = ffn_backward(
        after_cross, gains[2], ffn_in, ffn_out, kept_ffn, grad_out
    )
    grad_branch = grad_cross_out.astype(jnp.bfloat16)
    grad_out_proj = jnp.einsum(
        "rqd,rqe->de", grad_branch, attn_mixed, preferred_element_type=jnp.float32
    )
    grad_mixed = jnp.einsum(
        "rqd,de->rqe", grad_branch, out_proj, preferred_element_type=jnp.float32
    ).astype(jnp.bfloat16)
    grad_q, grad_k, grad_v = attention_backward(
        queries, keys_in, values_in, across, log_total, grad_mixed, head_count
    )
    grad_queries = grad_q.astype(jnp.bfloat16)
    grad_query_proj = outer_sum(normed, grad_queries)
    grad_normed = project_back(grad_queries, query_proj)
    _, norm_pull = jax.vjp(rms_norm, after_self, gains[1])
    grad_self_norm, grad_cross_gain = norm_pull(grad_normed)
    grad_after_self = grad_cross_out + grad_self_norm
    grad_hidden, grad_ai, grad_ao, grad_attn_gain = self_backward(
        hidden, gains[0], attn_in, attn_out, allowed, head_count, kept_attn, grad_after_self
    )
    grad_sent = jnp.concatenate([grad_k, grad_v], -1).astype(jnp.bfloat16)
    grad_cross = jnp.concatenate([grad_query_proj, grad_out_proj], -1)
    return (
        output,
        grad_hidden,
        grad_sent,
        (
            grad_ai,
            grad_ao,
            grad_fi,
            grad_fo,
            grad_cross,
            jnp.stack([grad_attn_gain, grad_cross_gain, grad_ffn_gain]),
        ),
    )


def owner_totals(received):
    totals = [jnp.sum(piece, 0) for piece in received]
    totals[5] = totals[5].T
    return tuple(totals)


def body(
    section_input, enc_lengths, dec_lengths, attn_in, attn_out, ffn_in, ffn_out, cross_weight, gains
):
    head_count = HEADS
    weights = (attn_in[0], attn_out[0], ffn_in[0], ffn_out[0], cross_weight[0], gains[0])
    enc_len = section_input.shape[2]
    dec_len = enc_len // 2
    seg_enc = segment_ids(enc_lengths, enc_len)
    seg_dec = segment_ids(dec_lengths, dec_len)
    batch_rows = section_input.shape[1] // MICRO
    on_decoder = lax.axis_index("section") == 1
    att_width = attn_out.shape[1]
    send_shape = (batch_rows, enc_len, 2 * att_width)

    def empty_grads():
        return (
            jnp.zeros(attn_in.shape[1:], jnp.float32),
            jnp.zeros(attn_out.shape[1:], jnp.float32),
            jnp.zeros(ffn_in.shape[1:], jnp.float32),
            jnp.zeros(ffn_out.shape[1:], jnp.float32),
            jnp.zeros(cross_weight.shape[1:], jnp.float32),
            jnp.zeros(gains.shape[1:], jnp.float32),
        )

    outgoing = jnp.zeros(send_shape, jnp.bfloat16)
    results = jnp.zeros(section_input.shape[1:], jnp.float32)
    grad_sums = empty_grads()
    shards = None
    for moment in range(MICRO + 2):
        if moment > 0:
            ahead = from_behind(outgoing, "section", 1)
            behind = from_behind(outgoing, "section", -1)
            incoming = jnp.where(on_decoder, ahead, behind)
        else:
            incoming = outgoing

        def encoder_moment(operand):
            arrived, collected = operand
            fresh = jnp.zeros(send_shape, jnp.bfloat16)
            pieces = empty_grads()
            if moment < MICRO:
                row_span = slice(moment * batch_rows, (moment + 1) * batch_rows)
                hidden = section_input[0, row_span].astype(jnp.float32)
                memory, _ = encoder_trunk(hidden, weights, seg_enc[row_span], head_count)
                fresh = project(memory, weights[4]).astype(jnp.bfloat16)
            if moment >= 2:
                row_span = slice((moment - 2) * batch_rows, (moment - 1) * batch_rows)
                hidden = section_input[0, row_span].astype(jnp.float32)
                grad_hidden, pieces = encoder_backward(
                    hidden, weights, seg_enc[row_span], head_count, arrived
                )
                collected = collected.at[row_span].set(grad_hidden)
            return (fresh, collected, pieces)

        def decoder_moment(operand):
            arrived, collected = operand
            if 1 <= moment <= MICRO:
                row_span = slice((moment - 1) * batch_rows, moment * batch_rows)
                dec_hidden = section_input[0, row_span, :dec_len].astype(jnp.float32)
                grad_out = section_input[0, row_span, dec_len:].astype(jnp.float32)
                output, grad_hidden, grad_sent, pieces = decoder_pass(
                    dec_hidden,
                    grad_out,
                    arrived,
                    weights,
                    seg_dec[row_span],
                    seg_enc[row_span],
                    head_count,
                )
                collected = collected.at[row_span].set(jnp.concatenate([output, grad_hidden], 1))
                return (grad_sent, collected, pieces)
            return (jnp.zeros(send_shape, jnp.bfloat16), collected, empty_grads())

        outgoing, results, pieces = lax.cond(
            on_decoder, decoder_moment, encoder_moment, (incoming, results)
        )
        grad_sums = tuple((older + newer for older, newer in zip(grad_sums, pieces)))
    received = (
        lax.all_to_all(
            grad_sums[0][None].astype(jnp.bfloat16), "rows", split_axis=1, concat_axis=0, tiled=True
        ).astype(jnp.float32),
        lax.all_to_all(
            grad_sums[1][None].astype(jnp.bfloat16), "rows", split_axis=1, concat_axis=0, tiled=True
        ).astype(jnp.float32),
        lax.all_to_all(
            grad_sums[2][None].astype(jnp.bfloat16), "rows", split_axis=1, concat_axis=0, tiled=True
        ).astype(jnp.float32),
        lax.all_to_all(
            grad_sums[3][None].astype(jnp.bfloat16), "rows", split_axis=1, concat_axis=0, tiled=True
        ).astype(jnp.float32),
        lax.all_to_all(
            grad_sums[4][None].astype(jnp.bfloat16), "rows", split_axis=1, concat_axis=0, tiled=True
        ).astype(jnp.float32),
        lax.all_to_all(
            grad_sums[5].T[None].astype(jnp.bfloat16),
            "rows",
            split_axis=1,
            concat_axis=0,
            tiled=True,
        ).astype(jnp.float32),
    )
    shards = owner_totals(received)
    return (
        results[None],
        shards[0][None],
        shards[1][None],
        shards[2][None],
        shards[3][None],
        shards[4][None],
        shards[5][None],
    )


def solution(mesh):
    placed = (
        P("section", "rows", None, None),
        P("rows", None),
        P("rows", None),
        P("section", None, None),
        P("section", None, None),
        P("section", None, None),
        P("section", None, None),
        P("section", None, None),
        P("section", None, None),
    )
    return jax.shard_map(
        body,
        mesh=mesh,
        in_specs=placed,
        out_specs=(
            P("section", "rows", None, None),
            P("section", "rows", None),
            P("section", "rows", None),
            P("section", "rows", None),
            P("section", "rows", None),
            P("section", "rows", None),
            P("section", None, "rows"),
        ),
        check_vma=False,
    )
```

profile of v0, /device:TPU:13, one launch (start us, length us, event | category | flops | bytes accessed | tf_op | source)
XLA Modules:
  0.0 1067.1 jit_solution(13007402193941200996)
XLA Ops:
  2.9 35.8 %conditional.4 = (f32[]{:T(128)}, bf16[1,512,1536]{1,2,0:T(8,128)(2,1)}) conditional(s32[]{:T(128)} %convert_element_type.789, (bf16[1,2,512,768]{3,2,1,0:T(8,128)(2,1)}, f32[3,768]{1,0:T(4,128)S(1)}, bf16[768,2304]{1,0:T(8,128)(2,1)}, s32[2,512]{1,0:T(2,128)}, bf16[768,768]{1,0:T(8,128)(2,1)}, /*index=5*/bf16[768,4096]{1,0:T(8,128)(2,1)}, ...), branch_computations={%region_4.10_spmd, %region_10.11_spmd} | conditional | flops 9300871168 | bytes 141677776 | solution.py:360
  4.8 4.3 fusion.15
  10.8 8.4 fusion.395
  19.6 5.9 fusion.31
  42.9 30.8 %collective-permute-done = bf16[1,512,1536]{1,2,0:T(8,128)(2,1)S(1)} collective-permute-done((bf16[1,512,1536]{1,2,0:T(8,128)(2,1)}, bf16[1,512,1536]{1,2,0:T(8,128)(2,1)S(1)}, u32[]{:S(2)}, u32[]{:S(2)}) %collective-permute-start) | collective-permute-done | bytes 1572896 | tf_op jit(solution)/shard_map/ppermute | solution.py:20
  77.4 57.3 %conditional.5 = (bf16[1,512,1536]{1,2,0:T(8,128)(2,1)}, f32[2,512,768]{2,1,0:T(8,128)}, f32[768,2304]{1,0:T(8,128)S(1)}, f32[768,768]{1,0:T(8,128)S(1)}, f32[76...) conditional(s32[]{:T(128)} %convert_element_type.789, ...), branch_computations={%region_11.17_spmd, %region_17.33_spmd} | conditional | flops 14586734592 | bytes 588748928 | solution.py:360
  84.8 7.9 fusion.397
  93.0 6.0 fusion.79
  134.8 47.0 %collective-permute-start.2 = (bf16[1,512,1536]{1,2,0:T(8,128)(2,1)}, bf16[1,512,1536]{1,2,0:T(8,128)(2,1)S(1)}, u32[]{:S(2)}, u32[]{:S(2)}) collective-permute-start(bf16[1,512,1536]{1,2,0:T(8,128)(2,1)} %get-tuple-element.269), channel_id=1, source_target_pairs={{0,16},{1,17},{2,18},{3,19},{4,20},{5,21},{6,22},{7,23},{8,24},{9,... | collective-permute-start | bytes 4718600 | tf_op jit(solution)/shard_map/ppermute | solution.py:20
  183.1 31.0 %collective-permute-done.2 = bf16[1,512,1536]{1,2,0:T(8,128)(2,1)S(1)} collective-permute-done((bf16[1,512,1536]{1,2,0:T(8,128)(2,1)}, bf16[1,512,1536]{1,2,0:T(8,128)(2,1)S(1)}, u32[]{:S(2)}, u32[]{:S(2)}) %collective-permute-start.2) | collective-permute-done | bytes 1572896 | tf_op jit(solution)/shard_map/ppermute | solution.py:20
  218.1 135.4 %conditional.6 = (f32[2,512,768]{2,1,0:T(8,128)}, f32[768,2304]{1,0:T(8,128)}, f32[768,768]{1,0:T(8,128)}, f32[768,4096]{1,0:T(8,128)}, f32[2048,768]{1,0:T(8,12...) conditional(s32[]{:T(128)} %convert_element_type.789, ...), branch_computations={%region_33.46_spmd, %region_46.62_spmd} | conditional | flops 26747076608 | bytes 604519360 | solution.py:360
  239.8 8.5 fusion.213
  261.3 6.5 bitcast_multiply_fusion.1
  267.8 7.1 multiply_reduce_fusion.13
  280.6 13.7 %multiply_reduce_fusion.12 = (f32[12,512]{1,0:T(8,128)S(1)}, f32[12,512,512]{1,2,0:T(8,128)}) fusion(f32[12,512]{1,0:T(8,128)S(1)} %log_add_fusion.2, f32[12,512,512]{1,2,0:T(8,128)} %copy-done, pred[512,512]{0,1:T(8,128)(4,1)S(1)} %broadcast_compare_fusion.3, bf16[512,12,64]{0,2,1:T(8,128)(2,1)} %bitcast.744, bf16[512,12,64]{0,2,1:T(8,128)(2,1)} %bitcast.741), kind=kOutput, calls=%fused_computation.260 | convolution fusion | flops 418375680 | bytes 27049984 | tf_op jit(solution)/shard_map/cond/branch_0_fun/rqhd,rkhd->rhqk/dot_general | solution.py:88
  294.3 7.1 multiply_convert_fusion.18
  310.5 9.2 fusion.218
  319.8 5.2 fusion.214
  325.0 4.5 fusion.225
  357.3 29.1 %collective-permute-done.4 = bf16[1,512,1536]{2,1,0:T(8,128)(2,1)} collective-permute-done((bf16[1,512,1536]{2,1,0:T(8,128)(2,1)}, bf16[1,512,1536]{2,1,0:T(8,128)(2,1)}, u32[]{:S(2)}, u32[]{:S(2)}) %collective-permute-start.4) | collective-permute-done | bytes 1572896 | tf_op jit(solution)/shard_map/ppermute | solution.py:20
  386.4 5.0 collective-permute-done.5
  391.4 109.5 %conditional.7 = (f32[768,2304]{1,0:T(8,128)}, f32[768,768]{1,0:T(8,128)}, f32[768,4096]{1,0:T(8,128)}, f32[2048,768]{1,0:T(8,128)}, f32[768,1536]{1,0:T(8,128)}...) conditional(s32[]{:T(128)} %convert_element_type.789, (bf16[1,2,512,768]{3,2,1,0:T(8,128)(2,1)}, ...), branch_computations={%region_62.75_spmd, %region_75.76_spmd} | conditional | flops 26748645376 | bytes 602380224 | solution.py:360
  392.8 4.3 fusion.336
  405.8 7.6 fusion.359
  425.8 8.8 bitcast_multiply_fusion.3
  434.6 6.5 multiply_reduce_fusion.28
  445.5 13.6 %multiply_reduce_fusion.27 = (f32[12,512]{1,0:T(8,128)S(1)}, f32[12,512,512]{1,2,0:T(8,128)}) fusion(f32[12,512]{1,0:T(8,128)S(1)} %log_add_fusion.5, f32[12,512,512]{1,2,0:T(8,128)} %copy-done.1, pred[512,512]{0,1:T(8,128)(4,1)S(1)} %broadcast_compare_fusion.5, bf16[512,12,64]{0,2,1:T(8,128)(2,1)} %bitcast.746, bf16[512,12,64]{0,2,1:T(8,128)(2,1)} %bitcast.743), kind=kOutput, calls=%fused_computation.495 | convolution fusion | flops 418375680 | bytes 27049984 | tf_op jit(solution)/shard_map/cond/branch_0_fun/rqhd,rkhd->rhqk/dot_general | solution.py:88
  459.2 7.1 multiply_convert_fusion.37
  477.1 6.6 fusion.364
  483.7 5.1 fusion.361
  488.8 4.5 fusion.371
  493.3 5.1 fusion.352
  502.0 10.1 all-to-all-start.5
  518.0 7.8 reduce.180
  527.0 6.5 all-to-all-start.1
  533.5 6.9 fusion.391
  540.4 5.7 copy.425
  546.1 15.7 %reduce.183 = bf16[768,1536]{1,0:T(8,128)(2,1)S(1)} reduce(bf16[768,1,1536]{2,1,0:T(2,128)(2,1)} %bitcast.690, bf16[]{:T(256)} %broadcast.1748), dimensions={1}, to_apply=%bitcast.649.reduce_sub_computation | reduce | bytes 4718594
  564.8 6.4 all-to-all-start.4
  571.2 7.7 fusion.390
  578.9 44.7 %copy.424 = bf16[1,2048,768]{2,0,1:T(2,128)(2,1)} copy(bf16[1,2048,768]{2,1,0:T(8,128)(2,1)S(1)} %fusion.390) | data formatting | bytes 6291456 | tf_op jit(solution)/shard_map/convert_element_type | solution.py:375
  623.6 31.6 %reduce.182 = bf16[2048,768]{1,0:T(8,128)(2,1)S(1)} reduce(bf16[2048,1,768]{2,1,0:T(2,128)(2,1)} %bitcast.687, bf16[]{:T(256)} %broadcast.1748), dimensions={1}, to_apply=%bitcast.648.reduce_sub_computation | reduce | bytes 6291458
  658.8 6.6 all-to-all-start.3
  665.4 8.4 fusion.389
  673.8 20.7 %copy.423 = bf16[1,768,2304]{2,0,1:T(2,128)(2,1)} copy(bf16[1,768,2304]{2,1,0:T(8,128)(2,1)S(1)} %fusion.389) | data formatting | bytes 7077888 | tf_op jit(solution)/shard_map/convert_element_type | solution.py:366
  694.6 75.2 %reduce.179 = bf16[768,2304]{1,0:T(8,128)(2,1)S(1)} reduce(bf16[768,1,2304]{2,1,0:T(2,128)(2,1)} %bitcast.686, bf16[]{:T(256)} %broadcast.1748), dimensions={1}, to_apply=%bitcast.647.reduce_sub_computation | reduce | bytes 7077890
  769.8 6.1 reshape.2814
  775.8 6.3 all-to-all-start
  782.1 13.3 %fusion.388 = bf16[1,768,4096]{2,1,0:T(8,128)(2,1)S(1)} fusion(f32[768,4096]{1,0:T(8,128)} %get-tuple-element.283, f32[768,4096]{1,0:T(8,128)} %get-tuple-element.282, f32[768,4096]{1,0:T(8,128)} %copy-done.4, f32[]{:T(128)} %get-tuple-element.274), kind=kLoop, calls=%fused_computation.601 | loop fusion | flops 12582912 | bytes 44040196 | tf_op jit(solution)/shard_map/convert_element_type | solution.py:372
  795.5 32.7 %copy.422 = bf16[1,768,4096]{2,0,1:T(2,128)(2,1)} copy(bf16[1,768,4096]{2,1,0:T(8,128)(2,1)S(1)} %fusion.388) | data formatting | bytes 12582912 | tf_op jit(solution)/shard_map/convert_element_type | solution.py:372
  828.2 40.0 %reduce.181 = bf16[768,4096]{1,0:T(8,128)(2,1)} reduce(bf16[768,1,4096]{2,1,0:T(2,128)(2,1)} %bitcast.681, bf16[]{:T(256)} %broadcast.1748), dimensions={1}, to_apply=%bitcast.646.reduce_sub_computation | reduce | bytes 12582914
  868.2 12.9 %reshape.2818 = bf16[16,2,98304]{2,1,0:T(2,128)(2,1)} reshape(bf16[768,4096]{1,0:T(8,128)(2,1)} %reduce.181) | data formatting | bytes 12582912
  881.1 6.0 all-to-all-start.2
  891.7 5.9 reshape.2817
  903.4 10.7 reshape.2823
  914.1 5.0 copy.414
  922.4 11.5 %reshape.2821 = bf16[2048,1,768]{2,1,0:T(2,128)(2,1)} reshape(bf16[16,2,49152]{2,1,0:T(2,128)(2,1)} %all-to-all-done.3) | data formatting | bytes 6291456
  933.8 5.9 copy.413
  943.6 7.9 reshape.2815
  951.6 6.4 copy.410
  962.1 62.4 %all-to-all-done.2 = bf16[16,2,98304]{2,1,0:T(2,128)(2,1)} async-done(((bf16[16,2,98304]{2,1,0:T(2,128)(2,1)}), bf16[16,2,98304]{2,1,0:T(2,128)(2,1)}, u32[]{:S(2)}, u32[]{:S(2)}) %all-to-all-start.2) | async-done | bytes 6291488 | tf_op jit(solution)/shard_map/all_to_all | solution.py:371
  1024.5 14.6 %reshape.2819 = bf16[768,1,4096]{2,1,0:T(2,128)(2,1)} reshape(bf16[16,2,98304]{2,1,0:T(2,128)(2,1)} %all-to-all-done.2) | data formatting | bytes 12582912
  1039.1 21.6 %copy.412 = f32[1,768,4096]{2,1,0:T(8,128)} copy(bf16[1,768,4096]{2,0,1:T(2,128)(2,1)} %bitcast.680) | data formatting | bytes 18874368
  1060.7 6.1 reduce_sum.639
  (337 shorter events, 196.2 us)
Async XLA Ops:
  19.5 7.0 slice-start
  19.6 6.0 copy-start.6
  19.6 6.0 copy-start.82
  19.6 7.2 slice-start.1
  38.6 35.0 %collective-permute-start = (bf16[1,512,1536]{1,2,0:T(8,128)(2,1)}, bf16[1,512,1536]{1,2,0:T(8,128)(2,1)S(1)}, u32[]{:S(2)}, u32[]{:S(2)}) collective-permute-start(bf16[1,512,1536]{1,2,0:T(8,128)(2,1)} %get-tuple-element.457), channel_id=1, source_target_pairs={{0,16},{1,17},{2,18},{3,19},{4,20},{5,21},{6,22},{7,23},{8,24},{9,... | collective-permute-start | bytes 4718600 | tf_op jit(solution)/shard_map/ppermute | solution.py:20
  40.0 37.4 %collective-permute-start.1 = (bf16[1,512,1536]{1,2,0:T(8,128)(2,1)}, bf16[1,512,1536]{1,2,0:T(8,128)(2,1)S(1)}, u32[]{:S(2)}, u32[]{:S(2)}) collective-permute-start(bf16[1,512,1536]{1,2,0:T(8,128)(2,1)} %get-tuple-element.457), channel_id=1, source_target_pairs={{16,0},{17,1},{18,2},{19,3},{20,4},{21,5},{22,6},{23,7},{24,8},{25... | collective-permute-start | bytes 4718600 | tf_op jit(solution)/shard_map/ppermute | solution.py:20
  93.0 7.0 slice-start.2
  93.0 6.0 copy-start.7
  93.0 6.0 copy-start.83
  93.0 7.2 slice-start.3
  134.7 83.4 %copy-start.4 = (f32[768,4096]{1,0:T(8,128)}, f32[768,4096]{1,0:T(8,128)S(1)}, u32[]{:S(2)}) copy-start(f32[768,4096]{1,0:T(8,128)S(1)} %get-tuple-element.281) | copy-start | bytes 37748740
  134.7 83.4 %copy-start.14 = (f32[768,2304]{1,0:T(8,128)}, f32[768,2304]{1,0:T(8,128)S(1)}, u32[]{:S(2)}) copy-start(f32[768,2304]{1,0:T(8,128)S(1)} %get-tuple-element.275) | copy-start | bytes 21233668
  134.7 83.4 %copy-start.19 = (f32[2048,768]{1,0:T(8,128)}, f32[2048,768]{1,0:T(8,128)S(1)}, u32[]{:S(2)}) copy-start(f32[2048,768]{1,0:T(8,128)S(1)} %get-tuple-element.284) | copy-start | bytes 18874372
  134.7 83.4 %copy-start.58 = (f32[768,768]{1,0:T(8,128)}, f32[768,768]{1,0:T(8,128)S(1)}, u32[]{:S(2)}) copy-start(f32[768,768]{1,0:T(8,128)S(1)} %get-tuple-element.278) | copy-start | bytes 7077892
  134.7 83.3 %copy-start.5 = (bf16[1,2,512,768]{3,2,1,0:T(8,128)(2,1)S(1)}, bf16[1,2,512,768]{3,2,1,0:T(8,128)(2,1)}, u32[]{:S(2)}) copy-start(bf16[1,2,512,768]{3,2,1,0:T(8,128)(2,1)} %param.25) | copy-start | bytes 4718596
  134.8 79.3 %collective-permute-start.2 = (bf16[1,512,1536]{1,2,0:T(8,128)(2,1)}, bf16[1,512,1536]{1,2,0:T(8,128)(2,1)S(1)}, u32[]{:S(2)}, u32[]{:S(2)}) collective-permute-start(bf16[1,512,1536]{1,2,0:T(8,128)(2,1)} %get-tuple-element.269), channel_id=1, source_target_pairs={{0,16},{1,17},{2,18},{3,19},{4,20},{5,21},{6,22},{7,23},{8,24},{9,... | collective-permute-start | bytes 4718600 | tf_op jit(solution)/shard_map/ppermute | solution.py:20
  181.8 36.2 %collective-permute-start.3 = (bf16[1,512,1536]{1,2,0:T(8,128)(2,1)}, bf16[1,512,1536]{1,2,0:T(8,128)(2,1)S(1)}, u32[]{:S(2)}, u32[]{:S(2)}) collective-permute-start(bf16[1,512,1536]{1,2,0:T(8,128)(2,1)} %get-tuple-element.269), channel_id=1, source_target_pairs={{16,0},{17,1},{18,2},{19,3},{20,4},{21,5},{22,6},{23,7},{24,8},{25... | collective-permute-start | bytes 4718600 | tf_op jit(solution)/shard_map/ppermute | solution.py:20
  218.4 89.4 %copy-start.184 = (f32[512]{0:T(512)}, f32[512]{0:T(512)S(1)}, u32[]{:S(2)}) copy-start(f32[512]{0:T(512)S(1)} %fusion.231) | copy-start | bytes 6148 | tf_op jit(solution)/shard_map/cond
  233.0 4.6 copy-start
  239.8 9.9 slice-start.6
  239.8 8.5 copy-start.86
  239.8 9.9 slice-start.7
  249.7 5.1 copy-start.78
  261.3 13.6 %copy-start.29 = (f32[512,768]{1,0:T(8,128)}, f32[512,768]{1,0:T(8,128)S(1)}, u32[]{:S(2)}) copy-start(f32[512,768]{1,0:T(8,128)S(1)} %add_add_fusion.5) | copy-start | bytes 4718596 | tf_op jit(solution)/shard_map/cond
  261.3 6.5 copy-start.79
  280.5 13.7 %slice-start.12 = ((s8[12582912]{0:T(1024)(128)(4,1)}), s8[4194304]{0:T(1024)(128)(4,1)S(1)}, s32[]{:S(2)}) async-start(s8[12582912]{0:T(1024)(128)(4,1)} %bitcast.669), calls=%async_computation.18 | async-start | bytes 8388608 | tf_op jit(solution)/shard_map/cond
  280.6 13.7 %slice-start.13 = ((s8[12582912]{0:T(1024)(128)(4,1)}), s8[4194304]{0:T(1024)(128)(4,1)S(1)}, s32[]{:S(2)}) async-start(s8[12582912]{0:T(1024)(128)(4,1)} %bitcast.669), calls=%async_computation.19 | async-start | bytes 8388608 | tf_op jit(solution)/shard_map/cond
  280.6 13.7 %slice-start.14 = ((s8[12582912]{0:T(1024)(128)(4,1)}), s8[4194304]{0:T(1024)(128)(4,1)S(1)}, s32[]{:S(2)}) async-start(s8[12582912]{0:T(1024)(128)(4,1)} %bitcast.669), calls=%async_computation.20 | async-start | bytes 8388608 | tf_op jit(solution)/shard_map/cond
  294.3 7.1 copy-start.43
  302.5 5.2 copy-start.109
  310.5 9.3 copy-start.110
  310.5 9.3 copy-start.139
  310.5 9.3 copy-start.185
  319.8 5.2 copy-start.30
  319.8 5.2 copy-start.49
  353.6 32.8 %collective-permute-start.4 = (bf16[1,512,1536]{2,1,0:T(8,128)(2,1)}, bf16[1,512,1536]{2,1,0:T(8,128)(2,1)}, u32[]{:S(2)}, u32[]{:S(2)}) collective-permute-start(bf16[1,512,1536]{2,1,0:T(8,128)(2,1)} %get-tuple-element.459), channel_id=1, source_target_pairs={{0,16},{1,17},{2,18},{3,19},{4,20},{5,21},{6,22},{7,23},{8,24},{9,... | collective-permute-start | bytes 4718600 | tf_op jit(solution)/shard_map/ppermute | solution.py:20
  356.0 35.3 %collective-permute-start.5 = (bf16[1,512,1536]{2,1,0:T(8,128)(2,1)}, bf16[1,512,1536]{2,1,0:T(8,128)(2,1)}, u32[]{:S(2)}, u32[]{:S(2)}) collective-permute-start(bf16[1,512,1536]{2,1,0:T(8,128)(2,1)} %get-tuple-element.459), channel_id=1, source_target_pairs={{16,0},{17,1},{18,2},{19,3},{20,4},{21,5},{22,6},{23,7},{24,8},{25... | collective-permute-start | bytes 4718600 | tf_op jit(solution)/shard_map/ppermute | solution.py:20
  391.4 109.5 %copy-start.155 = (f32[3,768]{1,0:T(4,128)S(1)}, f32[3,768]{1,0:T(4,128)}, u32[]{:S(2)}) copy-start(f32[3,768]{1,0:T(4,128)} %get-tuple-element.290) | copy-start | bytes 27652
  400.9 4.6 copy-start.1
  405.8 7.6 copy-start.102
  405.8 8.6 slice-start.10
  405.8 7.6 copy-start.13
  405.8 7.6 copy-start.90
  405.8 8.6 slice-start.11
  413.4 4.5 copy-start.134
  414.4 26.7 %copy-start.76 = (f32[512,768]{1,0:T(8,128)}, f32[512,768]{1,0:T(8,128)S(1)}, u32[]{:S(2)}) copy-start(f32[512,768]{1,0:T(8,128)S(1)} %get-tuple-element.591) | copy-start | bytes 4718596 | tf_op jit(solution)/shard_map/cond
  425.8 15.3 %copy-start.27 = (f32[512,768]{1,0:T(8,128)}, f32[512,768]{1,0:T(8,128)S(1)}, u32[]{:S(2)}) copy-start(f32[512,768]{1,0:T(8,128)S(1)} %add_add_fusion.11) | copy-start | bytes 4718596 | tf_op jit(solution)/shard_map/cond
  445.5 13.7 %slice-start.15 = ((s8[12582912]{0:T(1024)(128)(4,1)}), s8[4194304]{0:T(1024)(128)(4,1)S(1)}, s32[]{:S(2)}) async-start(s8[12582912]{0:T(1024)(128)(4,1)} %bitcast.671), calls=%async_computation.21 | async-start | bytes 8388608 | tf_op jit(solution)/shard_map/cond
  445.5 13.6 %slice-start.16 = ((s8[12582912]{0:T(1024)(128)(4,1)}), s8[4194304]{0:T(1024)(128)(4,1)S(1)}, s32[]{:S(2)}) async-start(s8[12582912]{0:T(1024)(128)(4,1)} %bitcast.671), calls=%async_computation.22 | async-start | bytes 8388608 | tf_op jit(solution)/shard_map/cond
  445.5 13.6 %slice-start.17 = ((s8[12582912]{0:T(1024)(128)(4,1)}), s8[4194304]{0:T(1024)(128)(4,1)S(1)}, s32[]{:S(2)}) async-start(s8[12582912]{0:T(1024)(128)(4,1)} %bitcast.671), calls=%async_computation.23 | async-start | bytes 8388608 | tf_op jit(solution)/shard_map/cond
  459.2 7.1 copy-start.42
  467.4 5.4 copy-start.107
  477.1 6.6 copy-start.108
  477.1 6.6 copy-start.137
  483.7 5.1 copy-start.28
  483.7 5.1 copy-start.47
  493.3 5.1 copy-start.135
  502.0 25.1 %all-to-all-start.5 = ((bf16[1,768,3]{2,0,1:T(2,128)(2,1)}), bf16[1,768,3]{2,0,1:T(2,128)(2,1)}, u32[]{:S(2)}, u32[]{:S(2)}) async-start(bf16[1,768,3]{2,0,1:T(2,128)(2,1)} %copy.376), calls=%async_computation.5 | async-start | bytes 786432 | tf_op jit(solution)/shard_map/all_to_all | solution.py:380
  527.0 37.8 %all-to-all-start.1 = ((bf16[16,2,18432]{2,1,0:T(2,128)(2,1)}), bf16[16,2,18432]{2,1,0:T(2,128)(2,1)S(1)}, u32[]{:S(2)}, u32[]{:S(2)}) async-start(bf16[16,2,18432]{2,1,0:T(2,128)(2,1)} %reshape.2816), calls=%async_computation.1 | async-start | bytes 2359296 | tf_op jit(solution)/shard_map/all_to_all | solution.py:368
  564.8 14.1 %copy-start.81 = (bf16[16,2,18432]{2,1,0:T(2,128)(2,1)}, bf16[16,2,18432]{2,1,0:T(2,128)(2,1)S(1)}, u32[]{:S(2)}) copy-start(bf16[16,2,18432]{2,1,0:T(2,128)(2,1)S(1)} %all-to-all-done.1) | copy-start | bytes 3538948
  564.8 94.0 %all-to-all-start.4 = ((bf16[16,2,36864]{2,1,0:T(2,128)(2,1)}), bf16[16,2,36864]{2,1,0:T(2,128)(2,1)}, u32[]{:S(2)}, u32[]{:S(2)}) async-start(bf16[16,2,36864]{2,1,0:T(2,128)(2,1)} %reshape.2822), calls=%async_computation.4 | async-start | bytes 4718592 | tf_op jit(solution)/shard_map/all_to_all | solution.py:377
  658.8 117.0 %all-to-all-start.3 = ((bf16[16,2,49152]{2,1,0:T(2,128)(2,1)}), bf16[16,2,49152]{2,1,0:T(2,128)(2,1)}, u32[]{:S(2)}, u32[]{:S(2)}) async-start(bf16[16,2,49152]{2,1,0:T(2,128)(2,1)} %reshape.2820), calls=%async_computation.3 | async-start | bytes 6291456 | tf_op jit(solution)/shard_map/all_to_all | solution.py:374
  775.8 105.3 %all-to-all-start = ((bf16[16,2,55296]{2,1,0:T(2,128)(2,1)}), bf16[16,2,55296]{2,1,0:T(2,128)(2,1)S(1)}, u32[]{:S(2)}, u32[]{:S(2)}) async-start(bf16[16,2,55296]{2,1,0:T(2,128)(2,1)} %reshape.2814), calls=%async_computation | async-start | bytes 7077888 | tf_op jit(solution)/shard_map/all_to_all | solution.py:365
  881.1 143.4 %all-to-all-start.2 = ((bf16[16,2,98304]{2,1,0:T(2,128)(2,1)}), bf16[16,2,98304]{2,1,0:T(2,128)(2,1)}, u32[]{:S(2)}, u32[]{:S(2)}) async-start(bf16[16,2,98304]{2,1,0:T(2,128)(2,1)} %reshape.2818), calls=%async_computation.2 | async-start | bytes 12582912 | tf_op jit(solution)/shard_map/all_to_all | solution.py:371
  (38 other events, 100.2 us)
where the time goes:
time: 1070 us
  local copies, waits for them, and re-layouts  273 us (26%)
  other arithmetic  267 us (25%)
  matrix products  230 us (21%)
  waiting for transfers between devices  166 us (16%)
  starting transfers between devices  96.5 us (9%)
  loops' own time  34 us (3%)
    unnamed x5, other arithmetic  170 us
    unnamed x31, local copies, waits for them, and re-layouts  121 us
    ppermute x6, waiting for transfers between devices, from_behind(): return lax.ppermute(x, axis, pairs)  103 us
    all_to_all x1, waiting for transfers between devices, body(): lax.all_to_all(grad_sums[2][None].astype(jnp.bfloat16), 'rows', split_axi...  62.4 us
    ppermute x6, starting transfers between devices, from_behind(): return lax.ppermute(x, axis, pairs)  54.7 us
    dot_general x18, matrix products, project(): jnp.einsum('rld,de->rle', left_op, right_op, preferred_element_type=jnp.f...  48.8 us
    convert_element_type x1, local copies, waits for them, and re-layouts, body(): grad_sums[3][None].astype(jnp.bfloat16)  44.7 us
    dot_general x9, matrix products, outer_sum(): jnp.einsum('rld,rle->de', left_op, grad_in, preferred_element_type=jnp.fl...  44.6 us
  transfers between devices with their start and end apart: 12, of which 7 were waited for; matrix products, arithmetic and copies ran while one was open for 39% of the time, Pallas kernels for 0%

commit v1 on v0

v1 whole, which is shorter than its diff:
```python
import functools

import jax
import jax.numpy as jnp
from jax import lax
from jax.experimental import pallas as pl
from jax.experimental.pallas import tpu as pltpu
from jax.sharding import PartitionSpec as P

HEADS = 12
HEAD = 64
PAIR = 128
EPSILON = 1e-06
SCALE = 0.125
LOG2E = 1.4426950408889634
NEGATIVE = -1e30
GELU_C = 0.7978845608028654
GELU_A = 0.044715

BF = jnp.bfloat16
F32 = jnp.float32
NT = (((1,), (1,)), ((), ()))
NN = (((1,), (0,)), ((), ()))
TN = (((0,), (0,)), ((), ()))


def mm(a, b, dims=NN):
    return lax.dot_general(a, b, dims, preferred_element_type=F32)


MESH = pl.DeviceIdType.MESH
LANES = 256
VMEM_LIMIT = 56 * 1024 * 1024

NZ, NY, NC = 4, 2, 2
Y_LAG = 2


def sum_scatter_kernel(counts, units, *refs):
    arrays = len(counts)
    ins, outs = refs[:arrays], refs[arrays : 2 * arrays]
    (own, got_core, got_y, got_r, got_l, s_local, s_core, r_core, s_y, r_y, s_r, r_r, s_l, r_l) = refs[
        2 * arrays :
    ]
    chunks = own.shape[0]
    sec, me = lax.axis_index("section"), lax.axis_index("rows")
    core, y, z = lax.rem(me, 2), lax.rem(me // 2, 2), me // 4
    by_core, by_y = me + 1 - 2 * core, me + 2 - 4 * y
    other, away = 1 - core, 1 - y

    barrier = pltpu.get_barrier_semaphore()

    def greet(peer):
        pl.semaphore_signal(barrier, inc=1, device_id=(sec, peer), device_id_type=MESH)

    greet(by_core)
    greet(by_y)

    @pl.when(z > 0)
    def _():
        greet(me - 4)

    @pl.when(z < NZ - 1)
    def _():
        greet(me + 4)

    @pl.when((z > 0) & (z < NZ - 1))
    def _():
        pl.semaphore_wait(barrier, 4)

    @pl.when((z == 0) | (z == NZ - 1))
    def _():
        pl.semaphore_wait(barrier, 3)

    def feed(src, dst_rows, chunk):
        pltpu.make_async_remote_copy(
            src_ref=src(other),
            dst_ref=got_core.at[chunk, :, :, dst_rows],
            send_sem=s_core.at[chunk],
            recv_sem=r_core.at[chunk],
            device_id=(sec, by_core),
            device_id_type=MESH,
        ).start()
        pltpu.make_async_copy(src(core), own.at[chunk, :, :, dst_rows], s_local.at[chunk]).start()

    base = 0
    for a in range(arrays):
        if units[a] is None:

            def panel(i, carry, a=a, base=base):
                at = pl.ds(pl.multiple_of(i * LANES, LANES), LANES)
                feed(lambda c: ins[a].at[:, :, c, :, at], pl.ds(0, own.shape[3]), base + i)
                return carry

            lax.fori_loop(0, counts[a], panel, 0)
        else:
            per = own.shape[3] // 16
            blocks = units[a]

            def unit(u, carry, a=a, base=base, blocks=blocks):
                at = pl.ds(pl.multiple_of((u // blocks) * LANES, LANES), LANES)
                rows_from = pl.ds(pl.multiple_of(lax.rem(u, blocks) * 16, 16), 16)
                rows_to = pl.ds(pl.multiple_of(lax.rem(u, per) * 16, 16), 16)
                feed(lambda c: ins[a].at[:, :, c, rows_from, at], rows_to, base + u // per)
                return carry

            lax.fori_loop(0, counts[a] * per, unit, 0)
        base += counts[a]

    def to_core(j):
        return pltpu.make_async_remote_copy(
            src_ref=got_core.at[j],
            dst_ref=got_core.at[j],
            send_sem=s_core.at[j],
            recv_sem=r_core.at[j],
            device_id=(sec, by_core),
            device_id_type=MESH,
        )

    def to_y(j):
        return pltpu.make_async_remote_copy(
            src_ref=own.at[j, :, away],
            dst_ref=got_y.at[j],
            send_sem=s_y.at[j],
            recv_sem=r_y.at[j],
            device_id=(sec, by_y),
            device_id_type=MESH,
        )

    def to_right(j, at):
        return pltpu.make_async_remote_copy(
            src_ref=own.at[j, pl.ds(at + 1, NZ - 1 - at), y],
            dst_ref=got_r.at[j, pl.ds(at + 1, NZ - 1 - at)],
            send_sem=s_r.at[j],
            recv_sem=r_r.at[j],
            device_id=(sec, me + 4),
            device_id_type=MESH,
        )

    def to_left(j, at):
        return pltpu.make_async_remote_copy(
            src_ref=own.at[j, pl.ds(0, at), y],
            dst_ref=got_l.at[j, pl.ds(0, at)],
            send_sem=s_l.at[j],
            recv_sem=r_l.at[j],
            device_id=(sec, me - 4),
            device_id_type=MESH,
        )

    def add_into(dst, src):
        dst[...] = (dst[...].astype(F32) + src[...].astype(F32)).astype(BF)

    def step(s, carry):
        @pl.when(s < chunks)
        def _():
            pltpu.make_async_copy(got_core.at[s], own.at[s], s_local.at[s]).wait()
            to_core(s).wait_recv()
            add_into(own.at[s], got_core.at[s])
            to_y(s).start()

        j_y = s - Y_LAG

        @pl.when((j_y >= 0) & (j_y < chunks))
        def _():
            to_y(j_y).wait_recv()
            for t in range(NZ):
                add_into(own.at[j_y, t, y], got_y.at[j_y, t])

        for at in range(NZ - 1):
            j_r = s - Y_LAG - at

            @pl.when((z == at) & (j_r >= 0) & (j_r < chunks))
            def _(at=at, j_r=j_r):
                if at > 0:
                    to_right(j_r, at - 1).wait_recv()
                    for t in range(at + 1, NZ):
                        add_into(own.at[j_r, t, y], got_r.at[j_r, t])
                to_right(j_r, at).start()

        for at in range(1, NZ):
            j_l = s - Y_LAG - (NZ - 1 - at)

            @pl.when((z == at) & (j_l >= 0) & (j_l < chunks))
            def _(at=at, j_l=j_l):
                if at < NZ - 1:
                    to_left(j_l, at + 1).wait_recv()
                    for t in range(at):
                        add_into(own.at[j_l, t, y], got_l.at[j_l, t])
                to_left(j_l, at).start()

        return carry

    lax.fori_loop(0, chunks + Y_LAG + NZ - 1, step, 0)

    def finish(j):
        for at in range(NZ):

            @pl.when(z == at)
            def _(at=at):
                if at == NZ - 1:
                    to_right(j, at - 1).wait_recv()
                if at == 0:
                    to_left(j, 1).wait_recv()
                to_y(j).wait_send()
                to_core(j).wait_send()
                if at < NZ - 1:
                    to_right(j, at).wait_send()
                if at > 0:
                    to_left(j, at).wait_send()

    def total(j, rows):
        mine = own[j, z, y, rows].astype(F32)
        right = got_r[j, z, rows].astype(F32)
        left = got_l[j, z, rows].astype(F32)
        return mine + jnp.where(z > 0, right, 0.0) + jnp.where(z < NZ - 1, left, 0.0)

    base = 0
    for a in range(arrays):
        if units[a] is None:

            def panel_out(i, carry, a=a, base=base):
                finish(base + i)
                at = pl.ds(pl.multiple_of(i * LANES, LANES), LANES)
                outs[a][:, at] = total(base + i, pl.ds(0, own.shape[3]))
                return carry

            lax.fori_loop(0, counts[a], panel_out, 0)
        else:
            per = own.shape[3] // 16
            blocks = units[a]

            def chunk_out(i, carry, base=base):
                finish(base + i)
                return carry

            lax.fori_loop(0, counts[a], chunk_out, 0)

            def unit_out(u, carry, a=a, base=base, blocks=blocks):
                at = pl.ds(pl.multiple_of((u // blocks) * LANES, LANES), LANES)
                rows_to = pl.ds(pl.multiple_of(lax.rem(u, blocks) * 16, 16), 16)
                rows_from = pl.ds(pl.multiple_of(lax.rem(u, per) * 16, 16), 16)
                outs[a][rows_to, at] = total(base + u // per, rows_from)
                return carry

            lax.fori_loop(0, counts[a] * per, unit_out, 0)
        base += counts[a]


def sum_scatter(pieces):
    peers = NZ * NY * NC
    height = min(p.shape[0] for p in pieces) // peers
    counts, units = [], []
    for p in pieces:
        rows = p.shape[0] // peers
        counts.append(rows * p.shape[1] // (height * LANES))
        units.append(None if rows == height else rows // 16)
    chunks = sum(counts)
    split = [p.reshape(NZ, NY, NC, p.shape[0] // peers, p.shape[1]) for p in pieces]
    half = (chunks, NZ, NY, height, LANES)
    fourth = (chunks, NZ, height, LANES)
    return pl.pallas_call(
        functools.partial(sum_scatter_kernel, tuple(counts), tuple(units)),
        in_specs=[pl.BlockSpec(memory_space=pl.ANY)] * len(pieces),
        out_specs=[pl.BlockSpec(memory_space=pltpu.VMEM)] * len(pieces),
        out_shape=[jax.ShapeDtypeStruct((p.shape[0] // peers, p.shape[1]), F32) for p in pieces],
        scratch_shapes=[
            pltpu.VMEM(half, BF),
            pltpu.VMEM(half, BF),
            pltpu.VMEM(fourth, BF),
            pltpu.VMEM(fourth, BF),
            pltpu.VMEM(fourth, BF),
        ]
        + [pltpu.SemaphoreType.DMA((chunks,))] * 9,
        compiler_params=pltpu.CompilerParams(
            collective_id=1, has_side_effects=True, vmem_limit_bytes=VMEM_LIMIT
        ),
    )(*split)


def low_half(rows):
    return lax.broadcasted_iota(jnp.int32, (rows, PAIR), 1) < HEAD


def masked_scores(q, k, qx, kx, head, causal):
    lo_q, lo_k = low_half(q.shape[0]), low_half(k.shape[0])
    if head == 0:
        qh, kh = jnp.where(lo_q, q, qx), jnp.where(lo_k, k, kx)
    else:
        qh, kh = jnp.where(lo_q, qx, q), jnp.where(lo_k, kx, k)
    s = mm(kh, qh, NT)
    if causal:
        key_at = lax.broadcasted_iota(jnp.int32, s.shape, 0)
        query_at = lax.broadcasted_iota(jnp.int32, s.shape, 1)
        s = jnp.where(key_at <= query_at, s, NEGATIVE)
    return s


def attn_fwd_kernel(q_ref, k_ref, v_ref, qx_ref, kx_ref, o_ref, lse_ref, *, causal):
    q, k, qx, kx = q_ref[0], k_ref[0], qx_ref[0], kx_ref[0]
    vt = v_ref[0].astype(F32).T.astype(BF)
    outs = []
    for head in range(2):
        s = masked_scores(q, k, qx, kx, head, causal)
        top = jnp.max(s, axis=0, keepdims=True)
        p = jnp.exp2((s - top) * (SCALE * LOG2E))
        total = jnp.sum(p, axis=0, keepdims=True)
        o = mm(vt[head * HEAD : (head + 1) * HEAD], p.astype(BF))
        outs.append(o / total)
        lse_ref[0, 0, head : head + 1, :] = top * (SCALE * LOG2E) + jnp.log2(total)
    o_ref[0] = jnp.concatenate(outs, axis=0).T.astype(BF)


def attn_bwd_kernel(
    q_ref, k_ref, v_ref, qx_ref, kx_ref, o_ref, do_ref, lse_ref, dq_ref, dk_ref, dv_ref, *, causal
):
    q, k, v, qx, kx = q_ref[0], k_ref[0], v_ref[0], qx_ref[0], kx_ref[0]
    do = do_ref[0]
    kt = k.astype(F32).T.astype(BF)
    spread = (do.astype(F32) * o_ref[0].astype(F32)).T
    lo_q, lo_k = low_half(q.shape[0]), low_half(k.shape[0])
    zero_q, zero_k = jnp.zeros_like(q), jnp.zeros_like(k)
    dqs, dk, dv = [], None, None
    for head in range(2):
        s = masked_scores(q, k, qx, kx, head, causal)
        p = jnp.exp2(s * (SCALE * LOG2E) - lse_ref[0, 0, head : head + 1, :])
        if head == 0:
            vh, doh, qh = (
                jnp.where(lo_k, v, zero_k),
                jnp.where(lo_q, do, zero_q),
                jnp.where(lo_q, q, zero_q),
            )
        else:
            vh, doh, qh = (
                jnp.where(lo_k, zero_k, v),
                jnp.where(lo_q, zero_q, do),
                jnp.where(lo_q, zero_q, q),
            )
        dp = mm(vh, do, NT)
        delta = jnp.sum(spread[head * HEAD : (head + 1) * HEAD], axis=0, keepdims=True)
        ds = (p * (dp - delta)).astype(BF)
        dv_part = mm(p.astype(BF), doh)
        dk_part = mm(ds, qh)
        dv = dv_part if dv is None else dv + dv_part
        dk = dk_part if dk is None else dk + dk_part
        dqs.append(mm(kt[head * HEAD : (head + 1) * HEAD], ds))
    dq_ref[0] = (jnp.concatenate(dqs, axis=0).T * SCALE).astype(BF)
    dk_ref[0] = (dk * SCALE).astype(BF)
    dv_ref[0] = dv.astype(BF)


def column_block(length, first):
    return pl.BlockSpec((1, length, PAIR), lambda r, p: (r, 0, first + p))


def whole_row(length):
    return pl.BlockSpec((1, length, PAIR), lambda r, p: (r, 0, 0))


def attention_forward(q_in, k_in, v_in, qx, kx, firsts, causal):
    rows, count_q, _ = q_in.shape
    count_k = k_in.shape[1]
    pairs = HEADS // 2
    return pl.pallas_call(
        functools.partial(attn_fwd_kernel, causal=causal),
        grid=(rows, pairs),
        in_specs=[
            column_block(count_q, firsts[0]),
            column_block(count_k, firsts[1]),
            column_block(count_k, firsts[2]),
            whole_row(count_q),
            whole_row(count_k),
        ],
        out_specs=[
            column_block(count_q, 0),
            pl.BlockSpec((1, 1, 2, count_q), lambda r, p: (r, p, 0, 0)),
        ],
        out_shape=[
            jax.ShapeDtypeStruct((rows, count_q, HEADS * HEAD), BF),
            jax.ShapeDtypeStruct((rows, pairs, 2, count_q), F32),
        ],
        compiler_params=pltpu.CompilerParams(vmem_limit_bytes=VMEM_LIMIT),
    )(q_in, k_in, v_in, qx, kx)


def attention_backward(q_in, k_in, v_in, qx, kx, firsts, mixed, grad_mixed, lse, causal):
    rows, count_q, _ = q_in.shape
    count_k = k_in.shape[1]
    pairs = HEADS // 2
    width = HEADS * HEAD
    return pl.pallas_call(
        functools.partial(attn_bwd_kernel, causal=causal),
        grid=(rows, pairs),
        in_specs=[
            column_block(count_q, firsts[0]),
            column_block(count_k, firsts[1]),
            column_block(count_k, firsts[2]),
            whole_row(count_q),
            whole_row(count_k),
            column_block(count_q, 0),
            column_block(count_q, 0),
            pl.BlockSpec((1, 1, 2, count_q), lambda r, p: (r, p, 0, 0)),
        ],
        out_specs=[
            column_block(count_q, 0),
            column_block(count_k, 0),
            column_block(count_k, 0),
        ],
        out_shape=[
            jax.ShapeDtypeStruct((rows, count_q, width), BF),
            jax.ShapeDtypeStruct((rows, count_k, width), BF),
            jax.ShapeDtypeStruct((rows, count_k, width), BF),
        ],
        compiler_params=pltpu.CompilerParams(vmem_limit_bytes=VMEM_LIMIT),
    )(q_in, k_in, v_in, qx, kx, mixed, grad_mixed, lse)


def segment_ids(lengths, span_len):
    seg_ends = jnp.cumsum(lengths, -1, dtype=jnp.int32)
    positions = jnp.arange(span_len, dtype=jnp.int32)
    return jnp.sum(
        (positions[None, :, None] >= seg_ends[:, None, :]).astype(jnp.int32), -1, dtype=jnp.int32
    )


def mask_lanes(seg, count):
    hit = seg[:, :, None] == jnp.arange(HEAD, dtype=jnp.int32)[None, None, :]
    member = hit.astype(BF)
    other = jnp.where(
        jnp.arange(HEAD, dtype=jnp.int32)[None, None, :] < count,
        jnp.where(hit, 0.0, NEGATIVE),
        0.0,
    ).astype(BF)
    return (
        jnp.concatenate([member, member], -1),
        jnp.concatenate([other, other], -1),
    )


def inverse_rms(v):
    return lax.rsqrt(jnp.mean(v * v, -1, keepdims=True) + EPSILON)


def norm(v, gain):
    return (v * inverse_rms(v) * gain).astype(BF)


def norm_back(v, gain, grad):
    inv = inverse_rms(v)
    scaled = grad * gain
    along = jnp.mean(scaled * v, -1, keepdims=True)
    return inv * scaled - v * (inv * inv * inv * along), jnp.sum(grad * v * inv, 0)


def gelu_parts(x):
    inner = GELU_C * (x + GELU_A * x * x * x)
    t = jnp.tanh(inner)
    value = 0.5 * x * (1.0 + t)
    slope = 0.5 * (1.0 + t) + 0.5 * x * (1.0 - t * t) * GELU_C * (1.0 + 3.0 * GELU_A * x * x)
    return value, slope


def ffn_forward(h, gain, w_in, w_out):
    m = norm(h, gain)
    u = mm(m, w_in)
    half = w_out.shape[0]
    value, _ = gelu_parts(u[:, :half])
    act = (value * u[:, half:]).astype(BF)
    return h + mm(act, w_out), (m, u.astype(BF), act)


def ffn_backward(h, gain, w_in, w_out, kept, grad):
    m, u, act = kept
    half = w_out.shape[0]
    branch = grad.astype(BF)
    d_act = mm(branch, w_out, NT)
    gate, up = u[:, :half].astype(F32), u[:, half:].astype(F32)
    value, slope = gelu_parts(gate)
    du = jnp.concatenate([d_act * up * slope, d_act * value], -1).astype(BF)
    dm = mm(du, w_in, NT)
    dh, dg = norm_back(h, gain, dm)
    return grad + dh, branch, du, dg


def shift(x, by):
    pairs = [(0, 1)] if by > 0 else [(1, 0)]
    return lax.ppermute(x, "section", pairs)


def body(
    section_input, enc_lengths, dec_lengths, attn_in, attn_out, ffn_in, ffn_out, cross_weight, gains
):
    wa, wo, wf, wd, wc = attn_in[0], attn_out[0], ffn_in[0], ffn_out[0], cross_weight[0]
    g0, g1, g2 = gains[0, 0], gains[0, 1], gains[0, 2]
    x_in = section_input[0]
    rows, le, dim = x_in.shape
    ld = le // 2
    width = wo.shape[0]
    docs = enc_lengths.shape[1]
    seg_enc = segment_ids(enc_lengths, le)
    seg_dec = segment_ids(dec_lengths, ld)
    enc_qx, enc_kx = mask_lanes(seg_enc, docs)
    dec_qx, dec_kx = mask_lanes(seg_dec, docs)
    on_decoder = lax.axis_index("section") == 1
    te, td = rows * le, rows * ld
    columns = width // PAIR
    own = (0, columns, 2 * columns)

    def self_forward(h, count, qx, kx, causal):
        n = norm(h, g0)
        packed = mm(n, wa).astype(BF)
        p3 = packed.reshape(rows, count, 3 * width)
        o, lse = attention_forward(p3, p3, p3, qx, kx, own, causal)
        o2 = o.reshape(rows * count, width)
        return h + mm(o2, wo), (n, packed, o, lse)

    def self_backward(h, count, qx, kx, causal, kept, grad):
        n, packed, o, lse = kept
        p3 = packed.reshape(rows, count, 3 * width)
        branch = grad.astype(BF)
        do = mm(branch, wo, NT).astype(BF).reshape(rows, count, width)
        dq, dk, dv = attention_backward(p3, p3, p3, qx, kx, own, o, do, lse, causal)
        dpacked = jnp.concatenate([dq, dk, dv], -1).reshape(rows * count, 3 * width)
        dn = mm(dpacked, wa, NT)
        dh, dg = norm_back(h, g0, dn)
        return grad + dh, branch, dpacked, dg

    def zeros(shape, dtype):
        return jnp.zeros(shape, dtype)

    def enc_first():
        h = x_in.reshape(te, dim).astype(F32)
        e1, (n, packed, o, lse) = self_forward(h, le, enc_qx, enc_kx, False)
        e2, (m, u, act) = ffn_forward(e1, g2, wf, wd)
        mem = norm(e2, g1)
        sent = mm(mem, wc).astype(BF)
        return (n, packed, o, lse, e1, m, u, act, e2, mem, sent, zeros((td, dim), BF))

    def dec_first():
        h = x_in[:, :ld].reshape(td, dim).astype(F32)
        d1, (n, packed, o, lse) = self_forward(h, ld, dec_qx, dec_kx, True)
        c = norm(d1, g1)
        cq = mm(c, wc[:, :width]).astype(BF)
        blank = jax.eval_shape(enc_first)

        def put(full, part):
            return lax.dynamic_update_slice(
                jnp.zeros(full.shape, full.dtype), part, (0,) * part.ndim
            )

        return (
            put(blank[0], n),
            put(blank[1], packed),
            put(blank[2], o),
            put(blank[3], lse),
            put(blank[4], d1),
            put(blank[5], c),
        ) + tuple(jnp.zeros(b.shape, b.dtype) for b in blank[6:11]) + (cq,)

    n, packed, o, lse, h1, m, u, act, e2, mem, sent, cq_out = lax.cond(
        on_decoder, dec_first, enc_first
    )
    cq = shift(cq_out, -1)

    def enc_cross():
        q3, s3 = cq.reshape(rows, ld, width), sent.reshape(rows, le, 2 * width)
        return tuple(
            attention_forward(q3, s3, s3, dec_qx, enc_kx, (0, 0, columns), False)
        )

    def dec_cross():
        return zeros((rows, ld, width), BF), zeros((rows, HEADS // 2, 2, ld), F32)

    oc_out, cross_lse = lax.cond(on_decoder, dec_cross, enc_cross)
    oc = shift(oc_out.reshape(td, width), 1)

    def enc_ffn():
        return (
            zeros((td, width), BF),
            zeros((td, dim), F32),
            zeros((td, dim), F32),
            zeros((td, dim), BF),
            zeros((td, wd.shape[0]), BF),
            zeros((td, dim), BF),
            zeros((td, wf.shape[1]), BF),
            zeros((td, dim), BF),
            zeros((dim,), F32),
        )

    def dec_ffn():
        d1 = h1[:td]
        d2 = d1 + mm(oc, wc[:, width:], NT)
        out, kept = ffn_forward(d2, g2, wf, wd)
        cot = x_in[:, ld:].reshape(td, dim).astype(F32)
        dd2, branch, du, dg = ffn_backward(d2, g2, wf, wd, kept, cot)
        cross_branch = dd2.astype(BF)
        doc = mm(cross_branch, wc[:, width:]).astype(BF)
        return doc, out, dd2, kept[0], kept[2], branch, du, cross_branch, dg

    doc_out, out, dd2, dec_m, dec_act, dec_branch, dec_du, cross_branch, dec_dg2 = lax.cond(
        on_decoder, dec_ffn, enc_ffn
    )
    doc = shift(doc_out, -1)

    def enc_cross_back():
        q3, s3 = cq.reshape(rows, ld, width), sent.reshape(rows, le, 2 * width)
        dq, dk, dv = attention_backward(
            q3, s3, s3, dec_qx, enc_kx, (0, 0, columns), oc_out,
            doc.reshape(rows, ld, width), cross_lse, False,
        )
        return dq, jnp.concatenate([dk, dv], -1).reshape(te, 2 * width)

    def dec_cross_back():
        return zeros((rows, ld, width), BF), zeros((te, 2 * width), BF)

    dcq_out, dsent = lax.cond(on_decoder, dec_cross_back, enc_cross_back)
    dcq = shift(dcq_out.reshape(td, width), 1)

    def enc_last():
        h = x_in.reshape(te, dim).astype(F32)
        dmem = mm(dsent, wc, NT)
        de2, dg1 = norm_back(e2, g1, dmem)
        de1, fbranch, du, dg2 = ffn_backward(h1, g2, wf, wd, (m, u, act), de2)
        dh, abranch, dpacked, dg0 = self_backward(
            h, le, enc_qx, enc_kx, False, (n, packed, o, lse), de1
        )
        return (
            dh.reshape(rows, le, dim),
            mm(n, dpacked, TN).astype(BF),
            mm(o.reshape(te, width), abranch, TN).astype(BF),
            mm(m, du, TN).astype(BF),
            mm(act, fbranch, TN).astype(BF),
            mm(mem, dsent, TN).astype(BF),
            jnp.stack([dg0, dg1, dg2]),
        )

    def dec_last():
        h = x_in[:, :ld].reshape(td, dim).astype(F32)
        d1, c = h1[:td], m[:td]
        dc = mm(dcq, wc[:, :width], NT)
        dd1_norm, dg1 = norm_back(d1, g1, dc)
        dd1 = dd2 + dd1_norm
        dn, dp, dox = n[:td], packed[:td], o[:, :ld]
        dlse = lse[..., :ld]
        dh, abranch, dpacked, dg0 = self_backward(
            h, ld, dec_qx, dec_kx, True, (dn, dp, dox, dlse), dd1
        )
        grad_cross = jnp.concatenate([mm(c, dcq, TN), mm(cross_branch, oc, TN)], -1)
        return (
            jnp.concatenate([out.reshape(rows, ld, dim), dh.reshape(rows, ld, dim)], 1),
            mm(dn, dpacked, TN).astype(BF),
            mm(dox.reshape(td, width), abranch, TN).astype(BF),
            mm(dec_m, dec_du, TN).astype(BF),
            mm(dec_act, dec_branch, TN).astype(BF),
            grad_cross.astype(BF),
            jnp.stack([dg0, dg1, dec_dg2]),
        )

    last = lax.cond(on_decoder, dec_last, enc_last)
    gain_terms = jnp.pad(last[6].T, ((0, 0), (0, LANES - last[6].shape[0]))).astype(BF)
    pieces = [last[1], last[2], last[3], last[5], gain_terms, last[4]]
    if lax.axis_size("rows") == NZ * NY * NC:
        sums = sum_scatter(pieces)
    else:
        sums = [
            lax.psum_scatter(piece, "rows", scatter_dimension=0, tiled=True).astype(F32)
            for piece in pieces
        ]
    s_in, s_out, s_fi, s_cross, s_gain, s_fo = sums
    return (
        last[0][None],
        s_in[None],
        s_out[None],
        s_fi[None],
        s_fo[None],
        s_cross[None],
        s_gain[:, : last[6].shape[0]].T[None],
    )


def solution(mesh):
    placed = (
        P("section", "rows", None, None),
        P("rows", None),
        P("rows", None),
    ) + (P("section", None, None),) * 6
    return jax.shard_map(
        body,
        mesh=mesh,
        in_specs=placed,
        out_specs=(
            P("section", "rows", None, None),
            P("section", "rows", None),
            P("section", "rows", None),
            P("section", "rows", None),
            P("section", "rows", None),
            P("section", "rows", None),
            P("section", None, "rows"),
        ),
        check_vma=False,
    )
```

time: 1070 us -> 482 us (0.45)
  the two profiles are of different devices: /device:TPU:13 before, /device:TPU:0 now
where the time goes in v1:
time: 482 us; the launch traced here: 473 us
  Pallas kernels  182 us (38%)
  matrix products  105 us (22%)
  waiting for transfers between devices  100 us (21%)
  local copies, waits for them, and re-layouts  41.6 us (9%)
  other arithmetic  30.3 us (6%)
  starting transfers between devices  6.09 us (1%)
  loops' own time  5.84 us (1%)
    pallas_call x1, Pallas kernels, sum_scatter(): pl.pallas_call(functools.partial(sum_scatter_kernel, tuple(counts), tuple...  114 us
    dot_general x15, matrix products, mm(): return lax.dot_general(a, b, dims, preferred_element_type=F32)  105 us
    ppermute x4, waiting for transfers between devices, shift(): return lax.ppermute(x, 'section', pairs)  100 us
    pallas_call x2, Pallas kernels, attention_backward(): pl.pallas_call(functools.partial(attn_bwd_kernel, causal=causal), grid=(r...  35.8 us
    pallas_call x2, Pallas kernels, attention_forward(): pl.pallas_call(functools.partial(attn_fwd_kernel, causal=causal), grid=(r...  32.7 us
    another operation x13, local copies, waits for them, and re-layouts  17.1 us
    unnamed x20, local copies, waits for them, and re-layouts  10.4 us
  transfers between devices with their start and end apart: 4, of which 4 were waited for; matrix products, arithmetic and copies ran while one was open for 0% of the time, Pallas kernels for 0%

profile of v1, /device:TPU:0, one launch (start us, length us, event | category | flops | bytes accessed | tf_op | source)
XLA Modules:
  0.0 472.8 jit_solution(14687490637160438799)
XLA Ops:
  0.6 0.9 reduce_window_sum.17
  4.9 0.9 add_convert_fusion
  5.9 71.8 %conditional.5 = (bf16[1024,768]{0,1:T(8,128)(2,1)S(1)}, bf16[1024,2304]{1,0:T(8,128)(2,1)}, bf16[2,512,768]{2,1,0:T(8,128)(2,1)}, f32[2,6,2,512]{3,2,1,0:T(2,12...) conditional(s32[]{:T(128)} %convert_element_type.188, ...), branch_computations={%region_4.8_spmd, %region_8.11_spmd} | conditional | flops 16955476992 | bytes 160529632 | solution.py:559
  6.6 3.7 copy.43
  10.3 1.7 multiply_reduce_fusion.2
  12.0 1.1 convert_element_type.193
  14.1 1.7 copy-done.42
  15.8 5.6 %convolution_convert_fusion = bf16[1024,2304]{1,0:T(8,128)(2,1)} fusion(bf16[1024,768]{0,1:T(8,128)(2,1)S(1)} %multiply_convert_fusion.2, bf16[768,2304]{1,0:T(8,128)(2,1)S(1)} %copy-done.42), kind=kOutput, calls=%fused_computation.8 | convolution fusion | flops 3626237952 | bytes 9830400 | tf_op jit(solution)/shard_map/cond/branch_0_fun/dot_general | solution.py:28
  21.4 17.9 %branch_0_fun.4 = (bf16[2,512,768]{2,1,0:T(8,128)(2,1)}, f32[2,6,2,512]{3,2,1,0:T(2,128)}) custom-call(bf16[2,512,2304]{2,1,0:T(8,128)(2,1)} %bitcast.q_ref.k_ref.v_ref, bf16[2,512,2304]{2,1,0:T(8,128)(2,1)} %bitcast.q_ref.k_ref.v_ref, bf16[2,512,2304]{2,1,0:T(8,128)(2,1)} %bitcast.q_ref.k_ref.v_ref, bf16[2,512,128]{2,1,0:T(8,128)(2,1)} %get-tuple-element.175.qx_ref, ...), custom_call_target="tpu_custom_call" | custom-call | tf_op jit(solution)/shard_map/cond/branch_0_fun/pallas_call | solution.py:363
  39.3 3.2 multiply_reduce_fusion.1
  42.5 1.5 multiply_convert_fusion.1
  44.0 11.6 %fusion.76 = (bf16[1024,4096]{1,0:T(8,128)(2,1)}, f32[1024,4096]{1,0:T(8,128)S(1)}) fusion(bf16[1024,768]{0,1:T(8,128)(2,1)} %multiply_convert_fusion.1, bf16[768,4096]{1,0:T(8,128)(2,1)} %get-tuple-element.181), kind=kOutput, calls=%fused_computation.194 | convolution fusion | flops 6446645248 | bytes 33030144 | tf_op jit(solution)/shard_map/cond/branch_0_fun/dot_general | solution.py:28
  55.6 4.3 fusion.5
  59.9 7.4 %multiply_reduce_fusion = (f32[1024]{0:T(1024)S(1)}, f32[1024,768]{0,1:T(8,128)}) fusion(f32[1024,768]{0,1:T(8,128)S(1)} %get-tuple-element.575, bf16[1024,2048]{1,0:T(8,128)(2,1)} %fusion.5, bf16[2048,768]{1,0:T(8,128)(2,1)S(1)} %copy-done.46), kind=kOutput, calls=%fused_computation.11 | convolution fusion | flops 3223583744 | bytes 13635584 | tf_op jit(solution)/shard_map/cond/branch_0_fun/dot_general | solution.py:28
  67.3 3.6 multiply_convert_fusion
  70.9 5.5 %convolution_convert_fusion.1 = bf16[1024,1536]{1,0:T(8,128)(2,1)} fusion(bf16[1024,768]{0,1:T(8,128)(2,1)} %multiply_convert_fusion, bf16[768,1536]{1,0:T(8,128)(2,1)S(1)} %copy-done.35), kind=kOutput, calls=%fused_computation.9 | convolution fusion | flops 2417491968 | bytes 7077888 | tf_op jit(solution)/shard_map/cond/branch_0_fun/dot_general | solution.py:28
  76.4 0.9 broadcast.315
  77.7 1.3 collective-permute-start
  79.0 20.7 %collective-permute-done = bf16[512,768]{1,0:T(8,128)(2,1)S(1)} collective-permute-done((bf16[512,768]{1,0:T(8,128)(2,1)}, bf16[512,768]{1,0:T(8,128)(2,1)S(1)}, u32[]{:S(2)}, u32[]{:S(2)}) %collective-permute-start) | collective-permute-done | bytes 786464 | tf_op jit(solution)/shard_map/ppermute | solution.py:486
  99.7 0.9 copy-done.22
  100.6 14.9 %conditional.6 = ((bf16[2,256,768]{2,1,0:T(8,128)(2,1)}, f32[2,6,2,256]{3,2,1,0:T(2,128)})) conditional(s32[]{:T(128)} %convert_element_type.188, (bf16[512,768]{1,0:T(8,128)(2,1)S(1)}, bf16[1024,1536]{1,0:T(8,128)(2,1)}, bf16[2,256,128]{2,1,0:T(8,128)(2,1)S(1)}, bf16[2,512,128]{2,1,0:T(8,128)(2,1)S(1)}) %tuple.62, () %tuple.63), branch_computations={%region_11.12_spmd, %region_12.13_spmd} | conditional | bytes 811038 | solution.py:573
  100.6 14.9 %branch_0_fun.5 = (bf16[2,256,768]{2,1,0:T(8,128)(2,1)}, f32[2,6,2,256]{3,2,1,0:T(2,128)}) custom-call(bf16[2,256,768]{2,1,0:T(8,128)(2,1)S(1)} %bitcast.203, bf16[2,512,1536]{2,1,0:T(8,128)(2,1)} %bitcast.6.k_ref.v_ref, bf16[2,512,1536]{2,1,0:T(8,128)(2,1)} %bitcast.6.k_ref.v_ref, bf16[2,256,128]{2,1,0:T(8,128)(2,1)S(1)} %get-tuple-element.197.qx_ref, ...), custom_call_target="tpu_custom_call" | custom-call | tf_op jit(solution)/shard_map/cond/branch_0_fun/pallas_call | solution.py:363
  115.5 2.2 collective-permute-start.1
  117.6 16.3 %collective-permute-done.1 = bf16[512,768]{1,0:T(8,128)(2,1)} collective-permute-done((bf16[512,768]{1,0:T(8,128)(2,1)}, bf16[512,768]{1,0:T(8,128)(2,1)}, u32[]{:S(2)}, u32[]{:S(2)}) %collective-permute-start.1) | collective-permute-done | bytes 786464 | tf_op jit(solution)/shard_map/ppermute | solution.py:486
  134.0 8.0 %conditional.7 = (bf16[512,768]{1,0:T(8,128)(2,1)S(1)}, f32[512,768]{1,0:T(8,128)S(1)}, f32[512,768]{1,0:T(8,128)S(1)}, bf16[512,768]{1,0:T(8,128)(2,1)}, bf16[5...) conditional(s32[]{:T(128)} %convert_element_type.188, () %tuple.61, ...), branch_computations={%region_13.14_spmd, %region_14.18_spmd} | conditional | flops 10927081472 | bytes 173841184 | solution.py:599
  134.5 0.9 broadcast.339.clone.2
  135.4 1.0 broadcast.339.clone.1
  136.4 1.0 broadcast.339.clone
  137.7 1.6 broadcast.341
  139.2 2.6 broadcast.342
  142.0 1.3 collective-permute-start.2
  143.3 47.6 %collective-permute-done.2 = bf16[512,768]{1,0:T(8,128)(2,1)S(1)} collective-permute-done((bf16[512,768]{1,0:T(8,128)(2,1)S(1)}, bf16[512,768]{1,0:T(8,128)(2,1)S(1)}, u32[]{:S(2)}, u32[]{:S(2)}) %collective-permute-start.2) | collective-permute-done | bytes 786464 | tf_op jit(solution)/shard_map/ppermute | solution.py:486
  190.9 15.9 %conditional.8 = (bf16[2,256,768]{2,1,0:T(8,128)(2,1)S(1)}, bf16[1024,1536]{1,0:T(8,128)(2,1)S(1)}) conditional(s32[]{:T(128)} %convert_element_type.188, (bf16[512,768]{1,0:T(8,128)(2,1)}, bf16[1024,1536]{1,0:T(8,128)(2,1)}, bf16[512,768]{1,0:T(8,128)(2,1)S(1)}, bf16[2,256,128]{2,1,0:T(8,128)(2,1)S(1)}, bf16[2,512,128]{2,1,0:T(8,128)(2,1)S(1)}, ...), branch_computations={%region_18.19_spmd, %region_19.20_spmd} | conditional | flops 6291456 | bytes 6291472 | solution.py:615
  190.9 13.8 %branch_0_fun.6 = (bf16[2,256,768]{2,1,0:T(8,128)(2,1)S(1)}, bf16[2,512,768]{2,1,0:T(8,128)(2,1)}, bf16[2,512,768]{2,1,0:T(8,128)(2,1)}) custom-call(bf16[2,256,768]{2,1,0:T(8,128)(2,1)} %bitcast.204, bf16[2,512,1536]{2,1,0:T(8,128)(2,1)} %bitcast.9.k_ref.v_ref, bf16[2,512,1536]{2,1,0:T(8,128)(2,1)} %bitcast.9.k_ref.v_ref, ...), custom_call_target="tpu_custom_call" | custom-call | tf_op jit(solution)/shard_map/cond/branch_0_fun/pallas_call | solution.py:390
  204.7 2.1 pad_maximum_fusion
  206.8 1.3 collective-permute-start.3
  208.2 15.7 %collective-permute-done.3 = bf16[512,768]{1,0:T(8,128)(2,1)S(1)} collective-permute-done((bf16[512,768]{1,0:T(8,128)(2,1)S(1)}, bf16[512,768]{1,0:T(8,128)(2,1)S(1)}, u32[]{:S(2)}, u32[]{:S(2)}) %collective-permute-start.3) | collective-permute-done | bytes 786464 | tf_op jit(solution)/shard_map/ppermute | solution.py:486
  223.9 124.4 %conditional.9 = (bf16[3,768]{1,0:T(4,128)(2,1)S(1)}, f32[1,2,512,768]{3,2,1,0:T(8,128)}, bf16[4,2,2,48,2304]{4,3,2,1,0:T(8,128)(2,1)}, bf16[4,2,2,48,768]{4,3,2...) conditional(s32[]{:T(128)} %convert_element_type.188, ...), branch_computations={%region_20.30_spmd, %region_30.37_spmd} | conditional | flops 33967466496 | bytes 307096480 | solution.py:658
  224.3 1.7 copy-done.23
  226.1 1.8 fusion.44
  227.9 6.4 %convolution_convert_fusion.7 = bf16[768,1536]{1,0:T(8,128)(2,1)} fusion(bf16[1024,768]{0,1:T(8,128)(2,1)} %get-tuple-element.499, bf16[1024,1536]{1,0:T(8,128)(2,1)} %copy-done.23), kind=kOutput, calls=%fused_computation.98 | convolution fusion | flops 2417098752 | bytes 7077888 | tf_op jit(solution)/shard_map/cond/branch_0_fun/dot_general | solution.py:28
  234.3 2.4 copy.46
  236.7 2.2 multiply_reduce_fusion.10
  238.9 2.4 copy.45
  241.6 1.6 copy-done.24
  243.1 4.6 multiply_reduce_fusion.8
  248.4 1.7 copy-done.6
  250.0 7.1 %fusion.50 = bf16[2048,768]{0,1:T(8,128)(2,1)} fusion(bf16[1024,2048]{1,0:T(8,128)(2,1)} %get-tuple-element.239, f32[1024,768]{1,0:T(8,128)S(1)} %multiply_subtract_fusion), kind=kOutput, calls=%fused_computation.118 | convolution fusion | flops 3223584768 | bytes 10485760 | tf_op jit(solution)/shard_map/cond/branch_0_fun/dot_general | solution.py:28
  257.1 4.8 %copy.61 = bf16[2048,768]{1,0:T(8,128)(2,1)} copy(bf16[2048,768]{0,1:T(8,128)(2,1)} %fusion.50) | data formatting | bytes 6291456 | tf_op jit(solution)/shard_map/cond | solution.py:658
  261.9 15.3 %fusion.37 = (bf16[1024,2048]{1,0:T(8,128)(2,1)}, bf16[1024,2048]{1,0:T(8,128)(2,1)}) fusion(bf16[1024,4096]{1,0:T(8,128)(2,1)} %get-tuple-element.226, bf16[2048,768]{1,0:T(8,128)(2,1)} %get-tuple-element.225, f32[1024,768]{1,0:T(8,128)} %copy-done.6), kind=kOutput, calls=%fused_computation.87 | convolution fusion | flops 3274440704 | bytes 23068672 | tf_op jit(solution)/shard_map/cond/branch_0_fun/dot_general | solution.py:28
  277.3 9.7 %multiply_reduce_fusion.9 = (f32[1024]{0:T(1024)S(1)}, bf16[768]{0:T(1024)(128)(2,1)S(1)}, f32[1024,768]{1,0:T(8,128)S(1)}) fusion(f32[1024,768]{1,0:T(8,128)S(1)} %copy-done.5, f32[768]{0:T(1024)S(1)} %reduce.11, f32[1024]{0:T(1024)S(1)} %add_rsqrt_fusion.4, bf16[768,4096]{1,0:T(8,128)(2,1)S(1)} %bitcast.196, bf16[1024,2048]{1,0:T(8,128)(2,1)} %get-tuple-element.555, ...), kind=kOutput, calls=%fused_computation.113 | convolution fusion | flops 6463944704 | bytes 20984320 | tf_op jit(solution)/shard_map/cond/branch_0_fun/dot_general | solution.py:28
  287.0 12.4 %convolution_convert_fusion.5 = bf16[4096,768]{0,1:T(8,128)(2,1)} fusion(bf16[1024,768]{0,1:T(8,128)(2,1)} %get-tuple-element.497, bf16[1024,2048]{1,0:T(8,128)(2,1)} %get-tuple-element.555, bf16[1024,2048]{1,0:T(8,128)(2,1)} %get-tuple-element.554), kind=kOutput, calls=%fused_computation.94 | convolution fusion | flops 6462373888 | bytes 16252928 | tf_op jit(solution)/shard_map/cond/branch_0_fun/dot_general | solution.py:28
  300.2 4.0 convolution_convert_fusion.10
  304.2 2.6 convolution_convert_fusion.9
  306.8 22.0 %branch_0_fun.7 = (bf16[2,512,768]{2,1,0:T(8,128)(2,1)}, bf16[2,512,768]{2,1,0:T(8,128)(2,1)}, bf16[2,512,768]{2,1,0:T(8,128)(2,1)}) custom-call(bf16[2,512,2304]{2,1,0:T(8,128)(2,1)} %bitcast.12.q_ref.k_ref.v_ref, bf16[2,512,2304]{2,1,0:T(8,128)(2,1)} %bitcast.12.q_ref.k_ref.v_ref, bf16[2,512,2304]{2,1,0:T(8,128)(2,1)} %bitcast.12.q_ref.k_ref.v_ref, ...), custom_call_target="tpu_custom_call" | custom-call | tf_op jit(solution)/shard_map/cond/branch_0_fun/pallas_call | solution.py:390
  328.8 2.6 pad_maximum_fusion.5
  331.6 5.5 %convolution_convert_fusion.6 = bf16[2304,768]{0,1:T(8,128)(2,1)} fusion(bf16[1024,768]{0,1:T(8,128)(2,1)S(1)} %copy-done.13, bf16[1024,2304]{1,0:T(8,128)(2,1)S(1)} %bitcast.201), kind=kOutput, calls=%fused_computation.96 | convolution fusion | flops 3625648128 | bytes 9830400 | tf_op jit(solution)/shard_map/cond/branch_0_fun/dot_general | solution.py:28
  337.2 4.2 fusion.47
  341.4 2.4 fusion.49
  349.3 113.6 %shard_map.144 = (f32[48,2304]{1,0:T(8,128)}, f32[48,768]{1,0:T(8,128)}, f32[48,4096]{1,0:T(8,128)}, f32[48,1536]{1,0:T(8,128)}, f32[48,256]{1,0:T(8,128)}, /*index=5*/f32[128,768]{1,0:T(8,128)}) custom-call(bf16[4,2,2,48,2304]{4,3,2,1,0:T(8,128)(2,1)} %get-tuple-element.339.refs_0_, bf16[4,2,2,48,768]{4,3,2,1,0:T(8,128)(2,1)} %get-tuple-element.340.refs_1_, ...), custom_call_target="tpu_custom_call" | custom-call | tf_op jit(solution)/shard_map/pallas_call | solution.py:261
  464.4 1.8 copy.143
  466.2 1.6 copy.144
  467.8 2.1 copy.145
  469.8 1.8 copy.146
  (87 shorter events, 11.0 us)
Async XLA Ops:
  13.8 2.0 copy-start.42
  39.3 3.3 copy-start.40
  55.6 4.3 copy-start.46
  67.3 3.6 copy-start.35
  77.7 22.0 %copy-start.12 = (bf16[1024,768]{0,1:T(8,128)(2,1)}, bf16[1024,768]{0,1:T(8,128)(2,1)S(1)}, u32[]{:S(2)}) copy-start(bf16[1024,768]{0,1:T(8,128)(2,1)S(1)} %get-tuple-element.325) | copy-start | bytes 4718596
  77.7 22.0 %collective-permute-start = (bf16[512,768]{1,0:T(8,128)(2,1)}, bf16[512,768]{1,0:T(8,128)(2,1)S(1)}, u32[]{:S(2)}, u32[]{:S(2)}) collective-permute-start(bf16[512,768]{1,0:T(8,128)(2,1)} %get-tuple-element.315), channel_id=1, source_target_pairs={{16,0},{17,1},{18,2},{19,3},{20,4},{21,5},{22,6},{23,7},{24,8},{25... | collective-permute-start | bytes 2359304 | tf_op jit(solution)/shard_map/ppermute | solution.py:486
  99.7 0.9 copy-start.22
  115.5 18.5 %collective-permute-start.1 = (bf16[512,768]{1,0:T(8,128)(2,1)}, bf16[512,768]{1,0:T(8,128)(2,1)}, u32[]{:S(2)}, u32[]{:S(2)}) collective-permute-start(bf16[512,768]{1,0:T(8,128)(2,1)} %bitcast.221), channel_id=1, source_target_pairs={{0,16},{1,17},{2,18},{3,19},{4,20},{5,21},{6,22},{7,23},{8,24},{9,... | collective-permute-start | bytes 2359304 | tf_op jit(solution)/shard_map/ppermute | solution.py:486
  142.0 49.0 %copy-start.14 = (f32[512,768]{1,0:T(8,128)}, f32[512,768]{1,0:T(8,128)S(1)}, u32[]{:S(2)}) copy-start(f32[512,768]{1,0:T(8,128)S(1)} %get-tuple-element.330) | copy-start | bytes 4718596
  142.0 49.0 %copy-start.16 = (f32[512,768]{1,0:T(8,128)}, f32[512,768]{1,0:T(8,128)S(1)}, u32[]{:S(2)}) copy-start(f32[512,768]{1,0:T(8,128)S(1)} %get-tuple-element.332) | copy-start | bytes 4718596
  142.0 48.9 %collective-permute-start.2 = (bf16[512,768]{1,0:T(8,128)(2,1)S(1)}, bf16[512,768]{1,0:T(8,128)(2,1)S(1)}, u32[]{:S(2)}, u32[]{:S(2)}) collective-permute-start(bf16[512,768]{1,0:T(8,128)(2,1)S(1)} %get-tuple-element.319), channel_id=1, source_target_pairs={{16,0},{17,1},{18,2},{19,3},{20,4},{21,5},{22,6},{23,7},{24,8},{25... | collective-permute-start | bytes 2359304 | tf_op jit(solution)/shard_map/ppermute | solution.py:486
  190.9 33.0 %copy-start.41 = (bf16[768]{0:T(1024)(128)(2,1)S(1)}, bf16[768]{0:T(1024)(128)(2,1)}, u32[]{:S(2)}) copy-start(bf16[768]{0:T(1024)(128)(2,1)} %get-tuple-element.331) | copy-start | bytes 4612
  206.8 17.0 %collective-permute-start.3 = (bf16[512,768]{1,0:T(8,128)(2,1)S(1)}, bf16[512,768]{1,0:T(8,128)(2,1)S(1)}, u32[]{:S(2)}, u32[]{:S(2)}) collective-permute-start(bf16[512,768]{1,0:T(8,128)(2,1)S(1)} %bitcast.248), channel_id=1, source_target_pairs={{0,16},{1,17},{2,18},{3,19},{4,20},{5,21},{6,22},{7,23},{8,24},{9,... | collective-permute-start | bytes 2359304 | tf_op jit(solution)/shard_map/ppermute | solution.py:486
  224.3 1.8 copy-start.23
  241.3 1.9 copy-start.24
  248.3 1.7 copy-start.6
  257.1 20.2 %slice-start.2 = ((s8[6291456]{0:T(1024)(128)(4,1)}), s8[2097152]{0:T(1024)(128)(4,1)S(1)}, s32[]{:S(2)}) async-start(s8[6291456]{0:T(1024)(128)(4,1)} %bitcast.195), calls=%async_computation.2 | async-start | bytes 4194304 | tf_op jit(solution)/shard_map/cond
  261.9 15.4 %copy-start.5 = (f32[1024,768]{1,0:T(8,128)S(1)}, f32[1024,768]{1,0:T(8,128)}, u32[]{:S(2)}) copy-start(f32[1024,768]{1,0:T(8,128)} %copy.46) | copy-start | bytes 9437188 | tf_op jit(solution)/shard_map/cond
  261.9 15.4 %slice-start.3 = ((s8[6291456]{0:T(1024)(128)(4,1)}), s8[4194304]{0:T(1024)(128)(4,1)S(1)}, s32[]{:S(2)}) async-start(s8[6291456]{0:T(1024)(128)(4,1)} %bitcast.195), calls=%async_computation.3 | async-start | bytes 8388608 | tf_op jit(solution)/shard_map/cond
  287.0 12.5 %copy-start.7 = (f32[1024,768]{1,0:T(8,128)S(1)}, f32[1024,768]{1,0:T(8,128)}, u32[]{:S(2)}) copy-start(f32[1024,768]{1,0:T(8,128)} %copy-done.6) | copy-start | bytes 9437188 | tf_op jit(solution)/shard_map/cond
  300.2 4.0 copy-start.31
  304.2 2.6 copy-start.38
  328.8 2.8 copy-start.13
  331.6 5.5 %copy-start.1 = (bf16[1,2,512,768]{3,2,1,0:T(8,128)(2,1)S(1)}, bf16[1,2,512,768]{3,2,1,0:T(8,128)(2,1)}, u32[]{:S(2)}) copy-start(bf16[1,2,512,768]{3,2,1,0:T(8,128)(2,1)} %get-tuple-element.235) | copy-start | bytes 4718596 | tf_op jit(solution)/shard_map/cond
  331.6 5.5 %copy-start.44 = (bf16[768,2304]{1,0:T(8,128)(2,1)S(1)}, bf16[768,2304]{1,0:T(8,128)(2,1)}, u32[]{:S(2)}) copy-start(bf16[768,2304]{1,0:T(8,128)(2,1)} %get-tuple-element.234) | copy-start | bytes 10616836 | tf_op jit(solution)/shard_map/cond
  463.0 8.6 %copy-start.37 = (f32[48,1536]{1,0:T(8,128)S(1)}, f32[48,1536]{1,0:T(8,128)}, u32[]{:S(2)}) copy-start(f32[48,1536]{1,0:T(8,128)} %get-tuple-element.349) | copy-start | bytes 884740
